TPU v7x, 768 devices: a whole 4x8x12 slice. The times are simulated.
768 devices in a mesh: band: 192 (over z, y, core), lon: 4 (over x).
Axes of the slice: x: 4, y: 8, z: 12, core: 2. Of those that a mesh axis runs over, the one named last changes fastest.
Arguments:
- thermal_state: bfloat16 [768, 8, 5136], P('band', None, 'lon'), may hold values from -6 to 6
- moisture_ratio: bfloat16 [768, 8, 5136], P('band', None, 'lon'), may hold values from 0 to 1
- ground_height_energy: bfloat16 [768, 5136], P('band', 'lon'), may hold values from -6 to 6
- column_summing_operator: float32 [8, 8], replicated, may hold values from -2 to 2
- polynomial_table: bfloat16 [768, 4, 192, 768], P('band', 'lon'), may hold values from -12 to 12
- parallel_angle_kept: int32 [768], P('band'), may hold values from 0 to 767, each once
- zonal_order_for_entry: int32 [768], P('band'), may hold values from 0 to 767, each once
- layer_for_entry: int32 [8], replicated, may hold values from 0 to 7, each once
Outputs:
- spectral: float32 [768, 2, 8, 768], P('band', None, 'lon')
Inputs may be any that keep to these rules, and one draw needn't show every extreme that they name: `parallel_angle_kept`: each latitude of the window is the latitude of exactly one stored row. `zonal_order_for_entry`: each zonal wavenumber is held in exactly one slot. `layer_for_entry`: each level is held in exactly one slot.
All inputs are finite; a program needn't handle non-finite values.
Results may differ from a plain program's by a relative error of at most 0.0049.
Values may be sent and summed in bfloat16 or wider, within the bound.
A program may use at most 64 MiB of HBM per device.

v0:
```python
import math

import jax
import jax.numpy as jnp
from jax import lax
from jax.sharding import PartitionSpec as P


def fourier_row(grid_row, length, wave_count):
    points = lax.iota(jnp.int32, grid_row.shape[1])
    wave_ids = lax.iota(jnp.int32, wave_count)
    residue = points[:, None] * wave_ids[None, :] % length
    angles = residue.astype(jnp.float32) * (2.0 * math.pi / length.astype(jnp.float32))
    inside = (points < length)[:, None]
    inverse = 1.0 / length.astype(jnp.float32)
    cos_table = jnp.where(inside, jnp.cos(angles) * inverse, 0.0).astype(jnp.bfloat16)
    sin_table = jnp.where(inside, -jnp.sin(angles) * inverse, 0.0).astype(jnp.bfloat16)
    tables = jnp.concatenate([cos_table, sin_table], axis=1)
    return jnp.dot(grid_row, tables, preferred_element_type=jnp.float32).astype(jnp.bfloat16)


def body(
    thermal_state,
    moisture_ratio,
    ground_height_energy,
    column_summing_operator,
    polynomial_table,
    parallel_angle_kept,
    zonal_order_for_entry,
    layer_for_entry,
):
    lat_count = lax.axis_size("band") * lax.axis_size("lon")
    lon_index = lax.axis_index("lon")
    wave_count = polynomial_table.shape[3]
    slot_count = zonal_order_for_entry.shape[0]
    density_thermal_state = thermal_state.astype(jnp.float32) * (
        1.0 + 0.608 * moisture_ratio.astype(jnp.float32)
    )
    geopotential = ground_height_energy.astype(jnp.float32)[:, None, :] + jnp.einsum(
        "gv,wvh->wgh",
        column_summing_operator,
        density_thermal_state,
        precision=lax.Precision.HIGHEST,
    )
    geopotential = geopotential.astype(jnp.bfloat16)
    whole_row = lax.all_to_all(geopotential, "lon", split_axis=0, concat_axis=2, tiled=True)
    latitude = lax.dynamic_index_in_dim(parallel_angle_kept, lon_index, 0, keepdims=False)
    distance = jnp.minimum(latitude, lat_count - 1 - latitude)
    length = whole_row.shape[2] - 4 * (lat_count // 2 - 1 - distance)
    spectrum = fourier_row(whole_row[0], length, wave_count)[None]
    columns = jnp.concatenate([zonal_order_for_entry, zonal_order_for_entry + wave_count])
    keep_mask = (
        lax.iota(jnp.int32, wave_count)[None, :] < (wave_count - zonal_order_for_entry)[:, None]
    ).astype(jnp.float32)
    own_plane = polynomial_table[:, 0]
    pieces = lax.all_gather(spectrum, "band", axis=0, tiled=True)
    chosen = jnp.take(pieces, columns, axis=2).reshape(
        pieces.shape[0], pieces.shape[1], 2, slot_count
    )
    partial_value = jnp.einsum(
        "srk,rlcs->sclk", own_plane, chosen, preferred_element_type=jnp.float32
    )
    partial_value = jnp.take(partial_value * keep_mask[:, None, None, :], layer_for_entry, axis=2)
    return lax.psum_scatter(partial_value, "lon", scatter_dimension=2, tiled=True)


def solution(mesh):
    placed = (
        P("band", None, "lon"),
        P("band", None, "lon"),
        P("band", "lon"),
        P(),
        P("band", "lon", None, None),
        P("band"),
        P("band"),
        P(),
    )
    return jax.shard_map(
        body, mesh=mesh, in_specs=placed, out_specs=P("band", None, "lon", None), check_vma=False
    )
```

profile of v0, /device:TPU:1, one launch (start us, length us, event | category | flops | bytes accessed | tf_op | source)
XLA Modules:
  0.0 448.8 jit_solution(7602910800949393719)
XLA Ops:
  6.5 0.0 copy-start
  6.5 0.8 convert_element_type.38
  7.3 1.9 fusion.11
  9.2 4.8 %all-to-all-start = ((bf16[4,8,1284]{2,1,0:T(8,128)(2,1)}), bf16[4,8,1284]{2,1,0:T(8,128)(2,1)S(1)}, u32[]{:S(2)}, u32[]{:S(2)}) async-start(bf16[4,8,1284]{2,1,0:T(8,128)(2,1)} %fusion.11), calls=%async_computation | async-start | bytes 180224 | tf_op jit(solution)/shard_map/all_to_all | solution.py:46
  14.1 0.0 all-gather.3.cloned.1.call-start
  14.1 1.2 dynamic_slice.4
  16.7 216.6 %select_convert_fusion.1 = (bf16[5136,768]{1,0:T(8,128)(2,1)}, bf16[5136,768]{1,0:T(8,128)(2,1)}) fusion(f32[]{:T(128)S(6)} %div.7, f32[]{:T(128)S(6)} %div.6, s32[]{:T(128)S(6)} %select_n.53, pred[5136]{0:T(1024)(128)(4,1)S(1)} %iota_compare_fusion, pred[]{:T(512)S(6)} %lt.65), kind=kLoop, calls=%fused_computation.10 | loop fusion | flops 67055616 | bytes 15782941 | tf_op jit(solution)/shard_map/convert_element_type | solution.py:16
  233.3 0.0 all-to-all-done
  233.3 0.1 squeeze.10
  233.5 0.0 copy-start.1
  233.5 0.0 copy-start.2
  233.5 7.7 %fusion.12 = bf16[8,1536]{1,0:T(8,128)(2,1)} fusion(bf16[8,5136]{1,0:T(8,128)(2,1)S(1)} %squeeze.10, bf16[5136,768]{1,0:T(8,128)(2,1)} %get-tuple-element.6, bf16[5136,768]{1,0:T(8,128)(2,1)} %get-tuple-element.5), kind=kOutput, calls=%fused_computation.19 | convolution fusion | flops 157790208 | bytes 15884544 | tf_op jit(solution)/shard_map/dot_general | solution.py:19
  241.2 0.0 all-gather.3.cloned.1.call-update
  241.2 0.0 all-reduce.3.cloned.1.call-start
  241.3 0.0 copy-done.1
  241.3 0.1 pad_add_fusion
  241.3 0.1 concatenate.36
  241.4 0.1 fusion.33
  241.5 0.0 copy-done.2
  241.6 0.1 fusion.31
  241.6 131.4 %all-gather.3.cloned.1.call-done = bf16[1536,1536]{1,0:T(8,128)(2,1)} async-done(((bf16[8,1536]{1,0:T(8,128)(2,1)}), bf16[1536,1536]{1,0:T(8,128)(2,1)}) %all-gather.3.cloned.1.call-update) | async-done | bytes 4718608 | tf_op jit(solution)/shard_map/all_gather | solution.py:56
  373.0 9.4 %copy.16 = bf16[192,8,1536]{0,1,2:T(8,128)(2,1)} copy(bf16[192,8,1536]{2,1,0:T(8,128)(2,1)} %bitcast.35) | data formatting | bytes 9437184 | tf_op jit(solution)/shard_map/all_gather | solution.py:56
  382.5 3.3 gather_fusion
  385.8 0.0 copy-done
  385.8 0.3 fusion.20
  386.1 0.1 copy.18
  386.3 0.7 gather_fusion.1
  386.9 0.8 select_bitcast_fusion
  387.7 0.0 all-reduce.3.cloned.1.call-update
  387.7 1.3 dynamic-slice
  389.7 50.8 %all-reduce.3.cloned.1.call-done = f32[4,2,8,768]{3,0,1,2:T(4,128)} async-done(((f32[4,2,8,768]{3,0,1,2:T(4,128)}), f32[4,2,8,768]{3,0,1,2:T(4,128)}) %all-reduce.3.cloned.1.call-update) | async-done | bytes 196624
  440.5 0.8 constant_dynamic-slice_fusion
  441.3 0.6 copy.19
  (8 shorter events, 0.1 us)
Async XLA Ops:
  6.5 379.3 %copy-start = (bf16[4,1,192,768]{3,2,1,0:T(8,128)(2,1)S(1)}, bf16[4,1,192,768]{3,2,1,0:T(8,128)(2,1)}, u32[]{:S(2)}) copy-start(bf16[4,1,192,768]{3,2,1,0:T(8,128)(2,1)} %param.12) | copy-start | bytes 3538948
  9.2 224.1 %all-to-all-start = ((bf16[4,8,1284]{2,1,0:T(8,128)(2,1)}), bf16[4,8,1284]{2,1,0:T(8,128)(2,1)S(1)}, u32[]{:S(2)}, u32[]{:S(2)}) async-start(bf16[4,8,1284]{2,1,0:T(8,128)(2,1)} %fusion.11), calls=%async_computation | async-start | bytes 180224 | tf_op jit(solution)/shard_map/all_to_all | solution.py:46
  14.1 359.0 %all-gather.3.cloned.1.call-start = ((), (), s32[]{:S(2)}) async-start(), calls=%async_computation.1 | async-start | bytes 4743168 | tf_op jit(solution)/shard_map/all_gather | solution.py:56
  233.5 7.8 %copy-start.1 = (s32[4]{0:T(128)S(1)}, s32[4]{0:T(128)}, u32[]{:S(2)}) copy-start(s32[4]{0:T(128)} %param.14) | copy-start | bytes 52
  233.5 8.1 %copy-start.2 = (s32[8]{0:T(128)S(1)}, s32[8]{0:T(128)}, u32[]{:S(2)}) copy-start(s32[8]{0:T(128)} %param.15) | copy-start | bytes 100
  241.2 199.3 %all-reduce.3.cloned.1.call-start = ((), (), s32[]{:S(2)}) async-start(), calls=%async_computation.2 | async-start | bytes 393216
Sparse Core Ops, SparseCore 0:
  241.3 131.6 all-gather.2
  387.9 52.6 all-reduce.2
where the time goes:
time: 450 us; the launch traced here: 449 us
  other arithmetic  218 us (48%)
  waiting for transfers between devices  182 us (40%)
  local copies, waits for them, and re-layouts  17.8 us (4%)
  between operations  15.6 us (3%)
  matrix products  9.88 us (2%)
  starting transfers between devices  4.89 us (1%)
    convert_element_type x1, other arithmetic, fourier_row(): jnp.where(inside, jnp.cos(angles) * inverse, 0.0).astype(jnp.bfloat16)  217 us
    all_gather x1, waiting for transfers between devices, body(): pieces = lax.all_gather(spectrum, 'band', axis=0, tiled=True)  131 us
    unnamed x3, waiting for transfers between devices  50.9 us
    all_gather x1, local copies, waits for them, and re-layouts, body(): pieces = lax.all_gather(spectrum, 'band', axis=0, tiled=True)  9.43 us
  transfers between devices with their start and end apart: 3, of which 2 were waited for; matrix products, arithmetic and copies ran while one was open for 49% of the time, Pallas kernels for 0%

commit v1 on v0

v1 whole, which is shorter than its diff:
```python
import jax
import jax.numpy as jnp
from jax import lax
from jax.experimental import pallas as pl
from jax.experimental.pallas import tpu as pltpu
from jax.sharding import PartitionSpec as P

Z, Y, CORES, LON = 12, 8, 2, 4
YC = Y * CORES
BANDS = Z * YC
LEVELS = 8
WAVES = 768
WIDEST = 5136
PIECE = WIDEST // LON
HALF = 768
BLOCK = 256
BLOCKS = LON * 2 * (HALF // BLOCK)
F32, BF16, I32 = jnp.float32, jnp.bfloat16, jnp.int32
MESH = pl.DeviceIdType.MESH

COS = (1.0, -4.93480110168457, 4.058692932128906, -1.335150122642517, 0.2350122481584549, -0.025341978296637535, 0.0015877870609983802)
SIN = (3.1415927410125732, -5.167712688446045, 2.5501599311828613, -0.5992405414581299, 0.08207812905311584, -0.007271677255630493, 0.000393970258301124)


def iota(shape, dim):
    return lax.broadcasted_iota(I32, shape, dim)


def circle(product, length, inverse):
    residue = product - jnp.round(product * inverse) * length
    x = residue * (inverse * 2.0)
    y = x * x
    c = COS[-1]
    s = SIN[-1]
    for a, b in zip(COS[-2::-1], SIN[-2::-1]):
        c = c * y + a
        s = s * y + b
    return c, s * x


def row_length(latitude):
    distance = jnp.minimum(latitude, LON * BANDS - 1 - latitude)
    return WIDEST - 4 * (LON * BANDS // 2 - 1 - distance)


def permuted_operator(operator, layers):
    t = iota((LEVELS, 1), 0)
    level = jnp.zeros((LEVELS, 1), I32)
    for i in range(LEVELS):
        level = jnp.where(t == i, layers[i], level)
    out = jnp.zeros((LEVELS, LEVELS), F32)
    for i in range(LEVELS):
        out = jnp.where(level == i, operator[i : i + 1, :], out)
    return out


def vertical_sum(temperature, moisture, ground, operator):
    virtual = temperature.astype(F32) * (1.0 + 0.608 * moisture.astype(F32))
    total = operator[:, 0:1] * virtual[0:1, :]
    for j in range(1, LEVELS):
        total = total + operator[:, j : j + 1] * virtual[j : j + 1, :]
    return total + ground.astype(F32)


def pack_piece(low, high, lon, length):
    both = jnp.concatenate([low, high], axis=0)
    point = lon * PIECE + jnp.where(iota((16, HALF), 0) >= 8, HALF, 0) + iota((16, HALF), 1)
    return jnp.where(point < length, both, 0.0).astype(BF16)


def phase_points():
    a = iota((BLOCKS, 128), 0)
    return ((a >> 3) * BLOCK + ((a >> 1) & 3) * PIECE + (a & 1) * HALF).astype(F32)


def legendre_row_of(row):
    return (row >> 2) & 3


def coefficient_order():
    r = iota((128, 128), 0)
    level = r & 7
    lane = (r & 64) + (level >> 1) * 16 + ((r >> 4) & 3) * 4 + ((r >> 3) & 1) * 2 + (level & 1)
    return jnp.where(lane == iota((128, 128), 1), 1.0, 0.0).astype(BF16)


def by_target():
    i = iota((128, 96), 0)
    source = (2 * (i & 7) + (i >> 6)) * Y + ((i >> 3) & 7)
    return jnp.where(source == iota((128, 96), 1), 1.0, 0.0).astype(BF16)


def by_band():
    i = iota((256, BANDS), 0)
    band = (2 * (i & 7) + (i >> 7)) * YC + ((i >> 3) & 15)
    return jnp.where(band == iota((256, BANDS), 1), 1.0, 0.0).astype(BF16)


def split_cores(rows):
    even, odd = rows[:64], rows[64:]
    first = iota((64, 128), 1) < 64
    return (
        jnp.where(first, even, pltpu.roll(odd, 64, 1)),
        jnp.where(first, pltpu.roll(even, 64, 1), odd),
    )


def dot(a, b):
    return jnp.dot(a, b, preferred_element_type=F32)


def kernel(
    latitudes, orders, layers, temperature, moisture, ground, operator, polynomial,
    out,
    t_in, q_in, g_in, o_in, p_in, fields, piece_out, piece_in, order_1, order_2, order_rows,
    tables, phases, columns, send_1, recv_1, send_2, recv_2, part_out, part_in,
    load_sem, send_sem, recv_sem,
):
    band, lon = lax.axis_index("band"), lax.axis_index("lon")
    z, yc = band // YC, band % YC
    y, core = yc // CORES, yc % CORES

    def over_z(o):
        return lax.rem(z + o, Z)

    def over_yc(o):
        return lax.rem(yc + o, YC)

    def over_lon(o):
        return lax.rem(lon + o, LON)

    barrier = pltpu.get_barrier_semaphore()
    for o in range(1, LON):
        pl.semaphore_signal(barrier, 1, device_id={"lon": over_lon(o)}, device_id_type=MESH)
    for o in range(1, YC):
        pl.semaphore_signal(barrier, 1, device_id={"band": z * YC + over_yc(o)}, device_id_type=MESH)
    for o in range(1, Z):
        pl.semaphore_signal(barrier, 1, device_id={"band": over_z(o) * YC + yc}, device_id_type=MESH)

    loads = [
        pltpu.make_async_copy(source, target, load_sem.at[i])
        for i, (source, target) in enumerate(
            ((temperature, t_in), (moisture, q_in), (ground, g_in), (operator, o_in), (polynomial.at[:, 0], p_in))
        )
    ]
    for load in loads:
        load.start()

    def exchange(stage, count, partner, source, target):
        for o in range(1, count):
            pltpu.make_async_remote_copy(
                src_ref=source(o), dst_ref=target, send_sem=send_sem.at[stage], recv_sem=recv_sem.at[stage],
                device_id=partner(o), device_id_type=MESH,
            ).start()

    def wait_recv(stage, ref):
        pltpu.make_async_copy(ref, ref, recv_sem.at[stage]).wait()

    def wait_send(stage, ref):
        pltpu.make_async_copy(ref, ref, send_sem.at[stage]).wait()

    def to_yc(o):
        return {"band": z * YC + over_yc(o)}

    def to_z(o):
        return {"band": over_z(o) * YC + yc}

    def to_lon(o):
        return {"lon": over_lon(o)}

    own_row, own_lane = iota((8, 128), 0) == y, iota((8, 128), 1) - core * 4
    tile = jnp.zeros((8, 128), F32)
    for s in range(4):
        tile = jnp.where(own_row & (own_lane == s), orders[s].astype(F32), tile)
    order_1[yc] = tile
    fields[:, :, 1280:] = jnp.zeros((4, LEVELS, 2 * HALF - 1280), F32)
    pl.semaphore_wait(barrier, LON + YC + Z - 3)
    exchange(0, YC, to_yc, lambda o: order_1.at[yc], order_1.at[yc])

    for load in loads[:4]:
        load.wait()
    operator_rows = permuted_operator(o_in[...], [layers[i] for i in range(LEVELS)])
    for r in range(4):
        fields[r, :, :PIECE] = vertical_sum(t_in[r], q_in[r], g_in[r : r + 1], operator_rows)
        piece_out[r] = pack_piece(fields[r, :, :HALF], fields[r, :, HALF:], lon, row_length(latitudes[r]))
    exchange(1, LON, to_lon, lambda o: piece_out.at[over_lon(o)], piece_in.at[lon])
    piece_in[lon] = piece_out[lon]

    wait_recv(0, order_1.at[pl.ds(0, YC - 1)])
    order_2[z] = jnp.sum(order_1[...], axis=0)
    order_2[pl.ds(Z, 4)] = jnp.zeros((4, 8, 128), F32)
    exchange(2, Z, to_z, lambda o: order_2.at[z], order_2.at[z])
    wait_recv(2, order_2.at[pl.ds(0, Z - 1)])
    order_rows[...] = order_2[...].reshape(128, 128).T[:8]

    length = jnp.full((1, 128), row_length(latitudes[lon]), I32).astype(F32)
    inverse = 1.0 / length

    def table(n, carry):
        m = order_rows[pl.ds(n, 1), :]
        step = iota((16, 128), 0).astype(F32)
        c0, s0 = circle(step * m, length, inverse)
        c1, s1 = circle(step * 16.0 * m, length, inverse)
        for b in range(16):
            c, s = c1[b : b + 1], s1[b : b + 1]
            tables[n, b * 16 : b * 16 + 16, :128] = (c * c0 - s * s0).astype(BF16)
            tables[n, b * 16 : b * 16 + 16, 128:] = (s * c0 + c * s0).astype(BF16)
        c, s = circle(phase_points() * m, length, inverse)
        phases[n, :, :128] = c * inverse
        phases[n, :, 128:] = s * inverse
        return carry

    lax.fori_loop(0, 8, table, 0)

    wait_recv(1, piece_in.at[pl.ds(0, LON - 1)])

    def transform(n, carry):
        c = jnp.zeros((8, 128), F32)
        s = jnp.zeros((8, 128), F32)
        for j in range(HALF // BLOCK):
            block = piece_in[:, :, j * BLOCK : (j + 1) * BLOCK].reshape(LON * 16, BLOCK)
            sums = dot(block, tables[n])
            for i in range(8):
                a = j * 8 + i
                pc, ps = phases[n, a : a + 1, :128], phases[n, a : a + 1, 128:]
                gc, gs = sums[i * 8 : i * 8 + 8, :128], sums[i * 8 : i * 8 + 8, 128:]
                c = c + (pc * gc - ps * gs)
                s = s - (ps * gc + pc * gs)
        columns[2 * n] = c
        columns[2 * n + 1] = s
        return carry

    lax.fori_loop(0, 8, transform, 0)

    turned = columns[...].reshape(128, 128).T.astype(BF16)
    send_1[...] = dot(turned, coefficient_order()).reshape(16, 8, 128)
    exchange(3, Z, to_z, lambda o: send_1.at[over_z(o)], recv_1.at[z])
    recv_1[z] = send_1[z]
    wait_recv(3, recv_1.at[pl.ds(0, Z - 1)])

    first, second = split_cores(dot(by_target(), recv_1[...].reshape(96, 128).astype(BF16)))
    for i in range(Y):
        send_2[2 * i] = first[i * 8 : i * 8 + 8]
        send_2[2 * i + 1] = second[i * 8 : i * 8 + 8]
    exchange(4, YC, to_yc, lambda o: send_2.at[over_yc(o)], recv_2.at[yc])
    recv_2[yc] = send_2[yc]
    loads[4].wait()
    wait_recv(4, recv_2.at[pl.ds(0, YC - 1)])

    turned = recv_2[...].reshape(128, 128).T.astype(BF16)
    rows = dot(jnp.concatenate([turned[:64], turned[64:]], axis=1), by_band())
    slot = legendre_row_of(iota((64, BANDS), 0))
    total = jnp.zeros((64, WAVES), F32)
    for s in range(4):
        total = total + dot(jnp.where(slot == s, rows, 0.0).astype(BF16), p_in[s])
    part_out[...] = total.reshape(LON, 16, WAVES)
    exchange(5, LON, to_lon, lambda o: part_out.at[over_lon(o)], part_in.at[lon])
    part_in[lon] = part_out[lon]
    wait_recv(5, part_in.at[pl.ds(0, LON - 1)])

    slot = legendre_row_of(iota((16, 1), 0))
    limit = jnp.zeros((16, 1), I32)
    for s in range(4):
        limit = jnp.where(slot == s, WAVES - orders[s], limit)
    summed = (part_in[0] + part_in[1]) + (part_in[2] + part_in[3])
    out[...] = jnp.where(iota((16, WAVES), 1) < limit, summed, 0.0)

    wait_send(0, order_1.at[pl.ds(0, YC - 1)])
    wait_send(1, piece_out.at[pl.ds(0, LON - 1)])
    wait_send(2, order_2.at[pl.ds(0, Z - 1)])
    wait_send(3, send_1.at[pl.ds(0, Z - 1)])
    wait_send(4, send_2.at[pl.ds(0, YC - 1)])
    wait_send(5, part_out.at[pl.ds(0, LON - 1)])


def body(temperature, moisture, ground, operator, polynomial, latitudes, orders, layers):
    anywhere = pl.BlockSpec(memory_space=pl.ANY)
    scalars = pl.BlockSpec(memory_space=pltpu.SMEM)
    vmem = pltpu.VMEM
    flat = pl.pallas_call(
        kernel,
        out_shape=jax.ShapeDtypeStruct((16, WAVES), F32),
        in_specs=[scalars] * 3 + [anywhere] * 5,
        out_specs=pl.BlockSpec(memory_space=pltpu.VMEM),
        scratch_shapes=[
            vmem(temperature.shape, BF16),
            vmem(moisture.shape, BF16),
            vmem(ground.shape, BF16),
            vmem(operator.shape, F32),
            vmem((4, BANDS, WAVES), BF16),
            vmem((4, LEVELS, 2 * HALF), F32),
            vmem((LON, 16, HALF), BF16),
            vmem((LON, 16, HALF), BF16),
            vmem((YC, 8, 128), F32),
            vmem((16, 8, 128), F32),
            vmem((8, 128), F32),
            vmem((8, BLOCK, 256), BF16),
            vmem((8, BLOCKS, 256), F32),
            vmem((16, 8, 128), F32),
            vmem((16, 8, 128), F32),
            vmem((Z, 8, 128), F32),
            vmem((YC, 8, 128), F32),
            vmem((YC, 8, 128), F32),
            vmem((LON, 16, WAVES), F32),
            vmem((LON, 16, WAVES), F32),
            pltpu.SemaphoreType.DMA((5,)),
            pltpu.SemaphoreType.DMA((6,)),
            pltpu.SemaphoreType.DMA((6,)),
        ],
        compiler_params=pltpu.CompilerParams(
            collective_id=0, has_side_effects=True, vmem_limit_bytes=32 * 1024 * 1024
        ),
    )(latitudes, orders, layers, temperature, moisture, ground, operator, polynomial)
    return flat.reshape(4, 2, 2, WAVES)


def solution(mesh):
    placed = (
        P("band", None, "lon"),
        P("band", None, "lon"),
        P("band", "lon"),
        P(),
        P("band", "lon", None, None),
        P("band"),
        P("band"),
        P(),
    )
    return jax.shard_map(
        body, mesh=mesh, in_specs=placed, out_specs=P("band", None, "lon", None), check_vma=False
    )
```

time: 450 us -> 57.5 us (0.13)
  other arithmetic: 218 us -> 0 us
  waiting for transfers between devices: 182 us -> 0 us
  Pallas kernels: 0 us -> 50.1 us
  between operations: 15.6 us -> 0.02 us
  local copies, waits for them, and re-layouts: 17.8 us -> 7.05 us
  matrix products: 9.88 us -> 0 us
  starting transfers between devices: 4.89 us -> 0 us
    convert_element_type x3 -> x0, other arithmetic: 217 us -> none  [the longest x1 217 us: fourier_row(): jnp.where(inside, jnp.cos(angles) * inverse, 0.0).astype(jnp.bfloat16)]
    all_gather x1 -> x0, waiting for transfers between devices: 131 us -> none  [body(): pieces = lax.all_gather(spectrum, 'band', axis=0, tiled=True)]
    unnamed x3 -> x0, waiting for transfers between devices: 50.9 us -> none
    pallas_call x0 -> x1, Pallas kernels: none -> 50.1 us  [body(): pl.pallas_call(kernel, out_shape=jax.ShapeDtypeStruct((16, WAVES), F32),...]
    dot_general x3 -> x0, matrix products: 9.88 us -> none  [the longest x1 7.69 us: fourier_row(): jnp.dot(grid_row, tables, preferred_element_type=jnp.float32)]
    all_gather x1 -> x0, local copies, waits for them, and re-layouts: 9.43 us -> none  [body(): pieces = lax.all_gather(spectrum, 'band', axis=0, tiled=True)]
    all_to_all x1 -> x0, starting transfers between devices: 4.84 us -> none  [body(): lax.all_to_all(geopotential, 'lon', split_axis=0, concat_axis=2, tiled=True)]
  transfers between devices with their start and end apart: 3 -> 0, of which waited for: 2 -> 0; matrix products, arithmetic and copies ran while one was open for 49% -> 0% of each run, Pallas kernels for 0% -> 0%
where the time goes in v1:
time: 57.5 us; the launch traced here: 57.1 us
  Pallas kernels  50.1 us (87%)
  local copies, waits for them, and re-layouts  7.05 us (12%)
    pallas_call x1, Pallas kernels, body(): pl.pallas_call(kernel, out_shape=jax.ShapeDtypeStruct((16, WAVES), F32),...  50.1 us
    unnamed x16, local copies, waits for them, and re-layouts  6.4 us

profile of v1, /device:TPU:1, one launch (start us, length us, event | category | flops | bytes accessed | tf_op | source)
XLA Modules:
  0.0 57.1 jit_solution(753994099719707752)
XLA Ops:
  0.0 0.0 copy-start
  0.0 1.3 %copy-done = bf16[4,1,192,768]{3,2,1,0:T(8,128)(2,1)S(1)} copy-done((bf16[4,1,192,768]{3,2,1,0:T(8,128)(2,1)S(1)}, bf16[4,1,192,768]{3,2,1,0:T(8,128)(2,1)}, u32[]{:S(2)}) %copy-start) | copy-done | bytes 1179672
  1.3 0.0 copy-start.1
  1.3 0.9 %copy-done.1 = bf16[4,8,1284]{2,1,0:T(8,128)(2,1)S(1)} copy-done((bf16[4,8,1284]{2,1,0:T(8,128)(2,1)S(1)}, bf16[4,8,1284]{2,1,0:T(8,128)(2,1)}, u32[]{:S(2)}) %copy-start.1) | copy-done | bytes 82200
  2.2 0.0 copy-start.2
  2.2 0.9 %copy-done.2 = bf16[4,8,1284]{2,1,0:T(8,128)(2,1)S(1)} copy-done((bf16[4,8,1284]{2,1,0:T(8,128)(2,1)S(1)}, bf16[4,8,1284]{2,1,0:T(8,128)(2,1)}, u32[]{:S(2)}) %copy-start.2) | copy-done | bytes 82200
  3.1 0.0 copy-start.3
  3.1 0.7 %copy-done.3 = bf16[4,1284]{1,0:T(4,128)(2,1)S(1)} copy-done((bf16[4,1284]{1,0:T(4,128)(2,1)S(1)}, bf16[4,1284]{1,0:T(4,128)(2,1)}, u32[]{:S(2)}) %copy-start.3) | copy-done | bytes 10296
  3.8 0.0 copy-start.4
  3.8 0.7 %copy-done.4 = f32[8,8]{1,0:T(8,128)S(1)} copy-done((f32[8,8]{1,0:T(8,128)S(1)}, f32[8,8]{1,0:T(8,128)}, u32[]{:S(2)}) %copy-start.4) | copy-done | bytes 280
  4.4 0.0 copy-start.5
  4.4 0.7 %copy-done.5 = s32[4]{0:T(128)S(1)} copy-done((s32[4]{0:T(128)S(1)}, s32[4]{0:T(128)}, u32[]{:S(2)}) %copy-start.5) | copy-done | bytes 40
  5.1 0.0 copy-start.6
  5.1 0.7 %copy-done.6 = s32[4]{0:T(128)S(1)} copy-done((s32[4]{0:T(128)S(1)}, s32[4]{0:T(128)}, u32[]{:S(2)}) %copy-start.6) | copy-done | bytes 40
  5.8 0.0 copy-start.7
  5.8 0.7 %copy-done.7 = s32[8]{0:T(128)S(1)} copy-done((s32[8]{0:T(128)S(1)}, s32[8]{0:T(128)}, u32[]{:S(2)}) %copy-start.7) | copy-done | bytes 56
  6.4 50.1 %shard_map.82 = f32[16,768]{1,0:T(8,128)S(1)} custom-call(s32[4]{0:T(128)S(1)} %copy-done.5, s32[4]{0:T(128)S(1)} %copy-done.6, s32[8]{0:T(128)S(1)} %copy-done.7, bf16[4,8,1284]{2,1,0:T(8,128)(2,1)S(1)} %copy-done.1, bf16[4,8,1284]{2,1,0:T(8,128)(2,1)S(1)} %copy-done.2, bf16[4,1284]{1,0:T(4,128)(2,1)S(1)} %copy-done.3, f32[8,8]{1,0:T(8,128)S(1)} %copy-done.4, ...), custom_call_target="tpu_custom_call" | custom-call | tf_op jit(solution)/shard_map/pallas_call | solution.py:280
  56.5 0.7 %reshape.3 = f32[4,2,2,768]{3,2,1,0:T(2,128)} reshape(f32[16,768]{1,0:T(8,128)S(1)} %shard_map.82) | data formatting | bytes 98304 | tf_op jit(solution)/shard_map/reshape | solution.py:314
Async XLA Ops:
  0.0 1.3 %copy-start = (bf16[4,1,192,768]{3,2,1,0:T(8,128)(2,1)S(1)}, bf16[4,1,192,768]{3,2,1,0:T(8,128)(2,1)}, u32[]{:S(2)}) copy-start(bf16[4,1,192,768]{3,2,1,0:T(8,128)(2,1)} %polynomial.1) | copy-start | bytes 3538948
  1.3 0.9 %copy-start.1 = (bf16[4,8,1284]{2,1,0:T(8,128)(2,1)S(1)}, bf16[4,8,1284]{2,1,0:T(8,128)(2,1)}, u32[]{:S(2)}) copy-start(bf16[4,8,1284]{2,1,0:T(8,128)(2,1)} %temperature.1) | copy-start | bytes 246532
  2.2 0.9 %copy-start.2 = (bf16[4,8,1284]{2,1,0:T(8,128)(2,1)S(1)}, bf16[4,8,1284]{2,1,0:T(8,128)(2,1)}, u32[]{:S(2)}) copy-start(bf16[4,8,1284]{2,1,0:T(8,128)(2,1)} %moisture.1) | copy-start | bytes 246532
  3.1 0.7 %copy-start.3 = (bf16[4,1284]{1,0:T(4,128)(2,1)S(1)}, bf16[4,1284]{1,0:T(4,128)(2,1)}, u32[]{:S(2)}) copy-start(bf16[4,1284]{1,0:T(4,128)(2,1)} %ground.1) | copy-start | bytes 30820
  3.8 0.7 %copy-start.4 = (f32[8,8]{1,0:T(8,128)S(1)}, f32[8,8]{1,0:T(8,128)}, u32[]{:S(2)}) copy-start(f32[8,8]{1,0:T(8,128)} %operator.1) | copy-start | bytes 772
  4.4 0.7 %copy-start.5 = (s32[4]{0:T(128)S(1)}, s32[4]{0:T(128)}, u32[]{:S(2)}) copy-start(s32[4]{0:T(128)} %latitudes.1) | copy-start | bytes 52
  5.1 0.7 %copy-start.6 = (s32[4]{0:T(128)S(1)}, s32[4]{0:T(128)}, u32[]{:S(2)}) copy-start(s32[4]{0:T(128)} %orders.1) | copy-start | bytes 52
  5.8 0.7 %copy-start.7 = (s32[8]{0:T(128)S(1)}, s32[8]{0:T(128)}, u32[]{:S(2)}) copy-start(s32[8]{0:T(128)} %layers.1) | copy-start | bytes 100

commit v2 on v1

--- a/solution.py
+++ b/solution.py
@@ -146,7 +146,10 @@
     for load in loads:
         load.start()
 
-    def exchange(stage, count, partner, source, target):
+    sent = []
+
+    def exchange(stage, count, partner, source, target, whole):
+        sent.append((stage, whole.at[pl.ds(0, count - 1)]))
         for o in range(1, count):
             pltpu.make_async_remote_copy(
                 src_ref=source(o), dst_ref=target, send_sem=send_sem.at[stage], recv_sem=recv_sem.at[stage],
@@ -156,8 +159,9 @@
     def wait_recv(stage, ref):
         pltpu.make_async_copy(ref, ref, recv_sem.at[stage]).wait()
 
-    def wait_send(stage, ref):
-        pltpu.make_async_copy(ref, ref, send_sem.at[stage]).wait()
+    def finish():
+        for stage, ref in sent:
+            pltpu.make_async_copy(ref, ref, send_sem.at[stage]).wait()
 
     def to_yc(o):
         return {"band": z * YC + over_yc(o)}
@@ -175,7 +179,7 @@
     order_1[yc] = tile
     fields[:, :, 1280:] = jnp.zeros((4, LEVELS, 2 * HALF - 1280), F32)
     pl.semaphore_wait(barrier, LON + YC + Z - 3)
-    exchange(0, YC, to_yc, lambda o: order_1.at[yc], order_1.at[yc])
+    exchange(0, YC, to_yc, lambda o: order_1.at[yc], order_1.at[yc], order_1)
 
     for load in loads[:4]:
         load.wait()
@@ -183,13 +187,13 @@
     for r in range(4):
         fields[r, :, :PIECE] = vertical_sum(t_in[r], q_in[r], g_in[r : r + 1], operator_rows)
         piece_out[r] = pack_piece(fields[r, :, :HALF], fields[r, :, HALF:], lon, row_length(latitudes[r]))
-    exchange(1, LON, to_lon, lambda o: piece_out.at[over_lon(o)], piece_in.at[lon])
+    exchange(1, LON, to_lon, lambda o: piece_out.at[over_lon(o)], piece_in.at[lon], piece_out)
     piece_in[lon] = piece_out[lon]
 
     wait_recv(0, order_1.at[pl.ds(0, YC - 1)])
     order_2[z] = jnp.sum(order_1[...], axis=0)
     order_2[pl.ds(Z, 4)] = jnp.zeros((4, 8, 128), F32)
-    exchange(2, Z, to_z, lambda o: order_2.at[z], order_2.at[z])
+    exchange(2, Z, to_z, lambda o: order_2.at[z], order_2.at[z], order_2)
     wait_recv(2, order_2.at[pl.ds(0, Z - 1)])
     order_rows[...] = order_2[...].reshape(128, 128).T[:8]
 
@@ -234,7 +238,7 @@
 
     turned = columns[...].reshape(128, 128).T.astype(BF16)
     send_1[...] = dot(turned, coefficient_order()).reshape(16, 8, 128)
-    exchange(3, Z, to_z, lambda o: send_1.at[over_z(o)], recv_1.at[z])
+    exchange(3, Z, to_z, lambda o: send_1.at[over_z(o)], recv_1.at[z], send_1)
     recv_1[z] = send_1[z]
     wait_recv(3, recv_1.at[pl.ds(0, Z - 1)])
 
@@ -242,7 +246,7 @@
     for i in range(Y):
         send_2[2 * i] = first[i * 8 : i * 8 + 8]
         send_2[2 * i + 1] = second[i * 8 : i * 8 + 8]
-    exchange(4, YC, to_yc, lambda o: send_2.at[over_yc(o)], recv_2.at[yc])
+    exchange(4, YC, to_yc, lambda o: send_2.at[over_yc(o)], recv_2.at[yc], send_2)
     recv_2[yc] = send_2[yc]
     loads[4].wait()
     wait_recv(4, recv_2.at[pl.ds(0, YC - 1)])
@@ -254,7 +258,7 @@
     for s in range(4):
         total = total + dot(jnp.where(slot == s, rows, 0.0).astype(BF16), p_in[s])
     part_out[...] = total.reshape(LON, 16, WAVES)
-    exchange(5, LON, to_lon, lambda o: part_out.at[over_lon(o)], part_in.at[lon])
+    exchange(5, LON, to_lon, lambda o: part_out.at[over_lon(o)], part_in.at[lon], part_out)
     part_in[lon] = part_out[lon]
     wait_recv(5, part_in.at[pl.ds(0, LON - 1)])
 
@@ -265,12 +269,7 @@
     summed = (part_in[0] + part_in[1]) + (part_in[2] + part_in[3])
     out[...] = jnp.where(iota((16, WAVES), 1) < limit, summed, 0.0)
 
-    wait_send(0, order_1.at[pl.ds(0, YC - 1)])
-    wait_send(1, piece_out.at[pl.ds(0, LON - 1)])
-    wait_send(2, order_2.at[pl.ds(0, Z - 1)])
-    wait_send(3, send_1.at[pl.ds(0, Z - 1)])
-    wait_send(4, send_2.at[pl.ds(0, YC - 1)])
-    wait_send(5, part_out.at[pl.ds(0, LON - 1)])
+    finish()
 
 
 def body(temperature, moisture, ground, operator, polynomial, latitudes, orders, layers):
@@ -308,7 +307,7 @@
             pltpu.SemaphoreType.DMA((6,)),
         ],
         compiler_params=pltpu.CompilerParams(
-            collective_id=0, has_side_effects=True, vmem_limit_bytes=32 * 1024 * 1024
+            collective_id=0, has_side_effects=True, vmem_limit_bytes=60 * 1024 * 1024
         ),
     )(latitudes, orders, layers, temperature, moisture, ground, operator, polynomial)
     return flat.reshape(4, 2, 2, WAVES)

time: 57.5 us -> 52.4 us (0.911)
  local copies, waits for them, and re-layouts: 7.05 us -> 1.45 us
  Pallas kernels: 50.1 us -> 50.8 us
    unnamed x16 -> x0, local copies, waits for them, and re-layouts: 6.4 us -> none
    reshape x1, local copies, waits for them, and re-layouts: 0.65 us -> 1.45 us  [body(): return flat.reshape(4, 2, 2, WAVES)]
    pallas_call x1, Pallas kernels: 50.1 us -> 50.8 us  [body(): pl.pallas_call(kernel, out_shape=jax.ShapeDtypeStruct((16, WAVES), F32),...]
where the time goes in v2:
time: 52.4 us; the launch traced here: 52.3 us
  Pallas kernels  50.8 us (97%)
  local copies, waits for them, and re-layouts  1.45 us (3%)
    pallas_call x1, Pallas kernels, body(): pl.pallas_call(kernel, out_shape=jax.ShapeDtypeStruct((16, WAVES), F32),...  50.8 us
    reshape x1, local copies, waits for them, and re-layouts, body(): return flat.reshape(4, 2, 2, WAVES)  1.45 us

profile of v2, /device:TPU:1, one launch (start us, length us, event | category | flops | bytes accessed | tf_op | source)
XLA Modules:
  0.0 52.3 jit_solution(6342650043472759524)
XLA Ops:
  0.0 50.8 %shard_map.82 = f32[16,768]{1,0:T(8,128)} custom-call(s32[4]{0:T(128)} %latitudes.1, s32[4]{0:T(128)} %orders.1, s32[8]{0:T(128)} %layers.1, bf16[4,8,1284]{2,1,0:T(8,128)(2,1)} %temperature.1, bf16[4,8,1284]{2,1,0:T(8,128)(2,1)} %moisture.1, bf16[4,1284]{1,0:T(4,128)(2,1)} %ground.1, f32[8,8]{1,0:T(8,128)} %operator.1, bf16[4,1,192,768]{3,2,1,0:T(8,128)(2,1)} %polynomial.1), custom_call_target="tpu_custom_call" | custom-call | tf_op jit(solution)/shard_map/pallas_call | solution.py:279
  50.8 1.4 %reshape.3 = f32[4,2,2,768]{3,2,1,0:T(2,128)} reshape(f32[16,768]{1,0:T(8,128)} %shard_map.82) | data formatting | bytes 98304 | tf_op jit(solution)/shard_map/reshape | solution.py:313

commit v3 on v2

--- a/solution.py
+++ b/solution.py
@@ -22,6 +22,10 @@
 SIN = (3.1415927410125732, -5.167712688446045, 2.5501599311828613, -0.5992405414581299, 0.08207812905311584, -0.007271677255630493, 0.000393970258301124)
 
 
+def far_first(count):
+    return sorted(range(count), key=lambda o: -min(o, count - o))
+
+
 def iota(shape, dim):
     return lax.broadcasted_iota(I32, shape, dim)
 
@@ -77,32 +81,11 @@
     return (row >> 2) & 3
 
 
-def coefficient_order():
-    r = iota((128, 128), 0)
-    level = r & 7
-    lane = (r & 64) + (level >> 1) * 16 + ((r >> 4) & 3) * 4 + ((r >> 3) & 1) * 2 + (level & 1)
-    return jnp.where(lane == iota((128, 128), 1), 1.0, 0.0).astype(BF16)
-
-
-def by_target():
-    i = iota((128, 96), 0)
-    source = (2 * (i & 7) + (i >> 6)) * Y + ((i >> 3) & 7)
-    return jnp.where(source == iota((128, 96), 1), 1.0, 0.0).astype(BF16)
-
-
-def by_band():
-    i = iota((256, BANDS), 0)
-    band = (2 * (i & 7) + (i >> 7)) * YC + ((i >> 3) & 15)
-    return jnp.where(band == iota((256, BANDS), 1), 1.0, 0.0).astype(BF16)
-
-
-def split_cores(rows):
-    even, odd = rows[:64], rows[64:]
-    first = iota((64, 128), 1) < 64
-    return (
-        jnp.where(first, even, pltpu.roll(odd, 64, 1)),
-        jnp.where(first, pltpu.roll(even, 64, 1), odd),
-    )
+def placement():
+    r, column = iota((16, 512), 0), iota((16, 512), 1)
+    slot, level = column >> 7, r & 7
+    lane = (level >> 1) * 16 + slot * 4 + (r >> 3) * 2 + (level & 1)
+    return jnp.where(lane == (column & 127), 1.0, 0.0).astype(BF16)
 
 
 def dot(a, b):
@@ -112,8 +95,8 @@
 def kernel(
     latitudes, orders, layers, temperature, moisture, ground, operator, polynomial,
     out,
-    t_in, q_in, g_in, o_in, p_in, fields, piece_out, piece_in, order_1, order_2, order_rows,
-    tables, phases, columns, send_1, recv_1, send_2, recv_2, part_out, part_in,
+    t_in, q_in, g_in, o_in, p_in, fields, piece_out, piece_in, order_1, order_2,
+    tables, phases, columns, row_out, row_in, part_out, part_in,
     load_sem, send_sem, recv_sem,
 ):
     band, lon = lax.axis_index("band"), lax.axis_index("lon")
@@ -130,12 +113,12 @@
         return lax.rem(lon + o, LON)
 
     barrier = pltpu.get_barrier_semaphore()
-    for o in range(1, LON):
+    for o in far_first(Z)[:-1]:
+        pl.semaphore_signal(barrier, 1, device_id={"band": over_z(o) * YC + yc}, device_id_type=MESH)
+    for o in far_first(LON)[:-1]:
         pl.semaphore_signal(barrier, 1, device_id={"lon": over_lon(o)}, device_id_type=MESH)
-    for o in range(1, YC):
+    for o in far_first(YC)[:-1]:
         pl.semaphore_signal(barrier, 1, device_id={"band": z * YC + over_yc(o)}, device_id_type=MESH)
-    for o in range(1, Z):
-        pl.semaphore_signal(barrier, 1, device_id={"band": over_z(o) * YC + yc}, device_id_type=MESH)
 
     loads = [
         pltpu.make_async_copy(source, target, load_sem.at[i])
@@ -150,7 +133,7 @@
 
     def exchange(stage, count, partner, source, target, whole):
         sent.append((stage, whole.at[pl.ds(0, count - 1)]))
-        for o in range(1, count):
+        for o in far_first(count)[:-1]:
             pltpu.make_async_remote_copy(
                 src_ref=source(o), dst_ref=target, send_sem=send_sem.at[stage], recv_sem=recv_sem.at[stage],
                 device_id=partner(o), device_id_type=MESH,
@@ -192,16 +175,13 @@
 
     wait_recv(0, order_1.at[pl.ds(0, YC - 1)])
     order_2[z] = jnp.sum(order_1[...], axis=0)
-    order_2[pl.ds(Z, 4)] = jnp.zeros((4, 8, 128), F32)
     exchange(2, Z, to_z, lambda o: order_2.at[z], order_2.at[z], order_2)
-    wait_recv(2, order_2.at[pl.ds(0, Z - 1)])
-    order_rows[...] = order_2[...].reshape(128, 128).T[:8]
 
     length = jnp.full((1, 128), row_length(latitudes[lon]), I32).astype(F32)
     inverse = 1.0 / length
 
     def table(n, carry):
-        m = order_rows[pl.ds(n, 1), :]
+        m = (n * 128 + iota((1, 128), 1)).astype(F32)
         step = iota((16, 128), 0).astype(F32)
         c0, s0 = circle(step * m, length, inverse)
         c1, s1 = circle(step * 16.0 * m, length, inverse)
@@ -214,7 +194,7 @@
         phases[n, :, 128:] = s * inverse
         return carry
 
-    lax.fori_loop(0, 8, table, 0)
+    lax.fori_loop(0, WAVES // 128, table, 0)
 
     wait_recv(1, piece_in.at[pl.ds(0, LON - 1)])
 
@@ -230,43 +210,70 @@
                 gc, gs = sums[i * 8 : i * 8 + 8, :128], sums[i * 8 : i * 8 + 8, 128:]
                 c = c + (pc * gc - ps * gs)
                 s = s - (ps * gc + pc * gs)
-        columns[2 * n] = c
-        columns[2 * n + 1] = s
+        turned = jnp.concatenate([c, s], axis=0).T.astype(BF16)
+        placed = dot(turned, placement()).astype(BF16)
+        for s in range(4):
+            columns[s, pl.ds(pl.multiple_of(n * 128, 128), 128), :] = placed[:, s * 128 : (s + 1) * 128]
         return carry
 
-    lax.fori_loop(0, 8, transform, 0)
-
-    turned = columns[...].reshape(128, 128).T.astype(BF16)
-    send_1[...] = dot(turned, coefficient_order()).reshape(16, 8, 128)
-    exchange(3, Z, to_z, lambda o: send_1.at[over_z(o)], recv_1.at[z], send_1)
-    recv_1[z] = send_1[z]
-    wait_recv(3, recv_1.at[pl.ds(0, Z - 1)])
-
-    first, second = split_cores(dot(by_target(), recv_1[...].reshape(96, 128).astype(BF16)))
-    for i in range(Y):
-        send_2[2 * i] = first[i * 8 : i * 8 + 8]
-        send_2[2 * i + 1] = second[i * 8 : i * 8 + 8]
-    exchange(4, YC, to_yc, lambda o: send_2.at[over_yc(o)], recv_2.at[yc], send_2)
-    recv_2[yc] = send_2[yc]
+    lax.fori_loop(0, WAVES // 128, transform, 0)
+
+    wait_recv(2, order_2.at[pl.ds(0, Z - 1)])
+    held = order_2[...].reshape(Z * Y, 128)
+    wave = iota((Z * Y, WAVES), 1).astype(F32)
+    for c in range(CORES):
+        rows = jnp.zeros((Z * Y, 128), F32)
+        for s in range(4):
+            i = c * 4 + s
+            chosen = jnp.where(held[:, i : i + 1] == wave, 1.0, 0.0).astype(BF16)
+            rows = rows + dot(chosen, columns[s])
+        row_out[c * Z * Y : (c + 1) * Z * Y] = rows.reshape(Z * Y, 1, 128)
+
+    def to_band(target_z, target_y, target_core):
+        pltpu.make_async_remote_copy(
+            src_ref=row_out.at[target_core * (Z * Y) + target_z * Y + target_y], dst_ref=row_in.at[band],
+            send_sem=send_sem.at[3], recv_sem=recv_sem.at[3],
+            device_id={"band": (target_z * Y + target_y) * CORES + target_core}, device_id_type=MESH,
+        ).start()
+
+    targets = []
+    for d in far_first(Y):
+        target_y = y + d
+        target_y = jnp.where(target_y >= Y, target_y - Y, target_y)
+        targets += [(target_y, 1 - core), (target_y, core)]
+
+    def to_other_z(i, carry):
+        half = (i + 1) // 2
+        target_z = z + Z // 2 + jnp.where(i % 2 == 1, -half, half)
+        target_z = jnp.where(target_z >= Z, target_z - Z, target_z)
+        for target in targets:
+            to_band(target_z, *target)
+        return carry
+
+    lax.fori_loop(0, Z - 1, to_other_z, 0)
+    for target in targets[:-1]:
+        to_band(z, *target)
+    sent.append((3, row_out.at[pl.ds(0, BANDS - 1)]))
+    row_in[band] = row_out[core * (Z * Y) + z * Y + y]
     loads[4].wait()
-    wait_recv(4, recv_2.at[pl.ds(0, YC - 1)])
-
-    turned = recv_2[...].reshape(128, 128).T.astype(BF16)
-    rows = dot(jnp.concatenate([turned[:64], turned[64:]], axis=1), by_band())
+    wait_recv(3, row_in.at[pl.ds(0, BANDS - 1)])
+
+    rows = row_in[...].reshape(BANDS, 128).T[:64]
     slot = legendre_row_of(iota((64, BANDS), 0))
     total = jnp.zeros((64, WAVES), F32)
     for s in range(4):
         total = total + dot(jnp.where(slot == s, rows, 0.0).astype(BF16), p_in[s])
-    part_out[...] = total.reshape(LON, 16, WAVES)
-    exchange(5, LON, to_lon, lambda o: part_out.at[over_lon(o)], part_in.at[lon], part_out)
+    part_out[...] = total.reshape(LON, 16, WAVES).astype(BF16)
+    exchange(4, LON, to_lon, lambda o: part_out.at[over_lon(o)], part_in.at[lon], part_out)
     part_in[lon] = part_out[lon]
-    wait_recv(5, part_in.at[pl.ds(0, LON - 1)])
+    wait_recv(4, part_in.at[pl.ds(0, LON - 1)])
 
     slot = legendre_row_of(iota((16, 1), 0))
     limit = jnp.zeros((16, 1), I32)
     for s in range(4):
         limit = jnp.where(slot == s, WAVES - orders[s], limit)
-    summed = (part_in[0] + part_in[1]) + (part_in[2] + part_in[3])
+    part = [part_in[i].astype(F32) for i in range(LON)]
+    summed = (part[0] + part[1]) + (part[2] + part[3])
     out[...] = jnp.where(iota((16, WAVES), 1) < limit, summed, 0.0)
 
     finish()
@@ -291,20 +298,17 @@
             vmem((LON, 16, HALF), BF16),
             vmem((LON, 16, HALF), BF16),
             vmem((YC, 8, 128), F32),
-            vmem((16, 8, 128), F32),
-            vmem((8, 128), F32),
-            vmem((8, BLOCK, 256), BF16),
-            vmem((8, BLOCKS, 256), F32),
-            vmem((16, 8, 128), F32),
-            vmem((16, 8, 128), F32),
             vmem((Z, 8, 128), F32),
-            vmem((YC, 8, 128), F32),
-            vmem((YC, 8, 128), F32),
-            vmem((LON, 16, WAVES), F32),
-            vmem((LON, 16, WAVES), F32),
+            vmem((WAVES // 128, BLOCK, 256), BF16),
+            vmem((WAVES // 128, BLOCKS, 256), F32),
+            vmem((4, WAVES, 128), BF16),
+            vmem((BANDS, 1, 128), F32),
+            vmem((BANDS, 1, 128), F32),
+            vmem((LON, 16, WAVES), BF16),
+            vmem((LON, 16, WAVES), BF16),
             pltpu.SemaphoreType.DMA((5,)),
-            pltpu.SemaphoreType.DMA((6,)),
-            pltpu.SemaphoreType.DMA((6,)),
+            pltpu.SemaphoreType.DMA((5,)),
+            pltpu.SemaphoreType.DMA((5,)),
         ],
         compiler_params=pltpu.CompilerParams(
             collective_id=0, has_side_effects=True, vmem_limit_bytes=60 * 1024 * 1024

time: 52.4 us -> 45.3 us (0.86)
  Pallas kernels: 50.8 us -> 43.7 us
    pallas_call x1, Pallas kernels: 50.8 us -> 43.7 us  [body(): pl.pallas_call(kernel, out_shape=jax.ShapeDtypeStruct((16, WAVES), F32),...]
where the time goes in v3:
time: 45.3 us; the launch traced here: 45.1 us
  Pallas kernels  43.7 us (96%)
  local copies, waits for them, and re-layouts  1.45 us (3%)
    pallas_call x1, Pallas kernels, body(): pl.pallas_call(kernel, out_shape=jax.ShapeDtypeStruct((16, WAVES), F32),...  43.7 us
    reshape x1, local copies, waits for them, and re-layouts, body(): return flat.reshape(4, 2, 2, WAVES)  1.45 us

profile of v3, /device:TPU:1, one launch (start us, length us, event | category | flops | bytes accessed | tf_op | source)
XLA Modules:
  0.0 45.1 jit_solution(5483173139049325657)
XLA Ops:
  0.0 43.7 %shard_map.82 = f32[16,768]{1,0:T(8,128)} custom-call(s32[4]{0:T(128)} %latitudes.1, s32[4]{0:T(128)} %orders.1, s32[8]{0:T(128)} %layers.1, bf16[4,8,1284]{2,1,0:T(8,128)(2,1)} %temperature.1, bf16[4,8,1284]{2,1,0:T(8,128)(2,1)} %moisture.1, bf16[4,1284]{1,0:T(4,128)(2,1)} %ground.1, f32[8,8]{1,0:T(8,128)} %operator.1, bf16[4,1,192,768]{3,2,1,0:T(8,128)(2,1)} %polynomial.1), custom_call_target="tpu_custom_call" | custom-call | tf_op jit(solution)/shard_map/pallas_call | solution.py:286
  43.7 1.4 %reshape.3 = f32[4,2,2,768]{3,2,1,0:T(2,128)} reshape(f32[16,768]{1,0:T(8,128)} %shard_map.82) | data formatting | bytes 98304 | tf_op jit(solution)/shard_map/reshape | solution.py:317

commit v4 on v3

--- a/solution.py
+++ b/solution.py
@@ -93,9 +93,9 @@
 
 
 def kernel(
-    latitudes, orders, layers, temperature, moisture, ground, operator, polynomial,
+    latitudes_at, orders_at, layers_at, temperature, moisture, ground, operator, polynomial,
     out,
-    t_in, q_in, g_in, o_in, p_in, fields, piece_out, piece_in, order_1, order_2,
+    latitudes, orders, layers, t_in, q_in, g_in, o_in, p_in, fields, piece_out, piece_in, order_1, order_2,
     tables, phases, columns, row_out, row_in, part_out, part_in,
     load_sem, send_sem, recv_sem,
 ):
@@ -123,7 +123,10 @@
     loads = [
         pltpu.make_async_copy(source, target, load_sem.at[i])
         for i, (source, target) in enumerate(
-            ((temperature, t_in), (moisture, q_in), (ground, g_in), (operator, o_in), (polynomial.at[:, 0], p_in))
+            (
+                (orders_at, orders), (layers_at, layers), (latitudes_at, latitudes),
+                (operator, o_in), (temperature, t_in), (moisture, q_in), (ground, g_in), (polynomial.at[:, 0], p_in),
+            )
         )
     ]
     for load in loads:
@@ -155,16 +158,18 @@
     def to_lon(o):
         return {"lon": over_lon(o)}
 
-    own_row, own_lane = iota((8, 128), 0) == y, iota((8, 128), 1) - core * 4
-    tile = jnp.zeros((8, 128), F32)
+    loads[0].wait()
+    lane = iota((1, 128), 1)
+    row = jnp.zeros((1, 128), I32)
     for s in range(4):
-        tile = jnp.where(own_row & (own_lane == s), orders[s].astype(F32), tile)
-    order_1[yc] = tile
+        digit = jnp.where(lane < 64, orders[s] & ~31, orders[s] & 31)
+        row = jnp.where((lane & 63) == yc * 4 + s, digit, row)
+    order_1[yc] = row.astype(F32)
     fields[:, :, 1280:] = jnp.zeros((4, LEVELS, 2 * HALF - 1280), F32)
     pl.semaphore_wait(barrier, LON + YC + Z - 3)
     exchange(0, YC, to_yc, lambda o: order_1.at[yc], order_1.at[yc], order_1)
 
-    for load in loads[:4]:
+    for load in loads[1:7]:
         load.wait()
     operator_rows = permuted_operator(o_in[...], [layers[i] for i in range(LEVELS)])
     for r in range(4):
@@ -219,7 +224,9 @@
     lax.fori_loop(0, WAVES // 128, transform, 0)
 
     wait_recv(2, order_2.at[pl.ds(0, Z - 1)])
-    held = order_2[...].reshape(Z * Y, 128)
+    own = ((iota((Y, 128), 1) & 63) >> 3) == iota((Y, 128), 0)
+    digits = jnp.concatenate([jnp.where(own, order_2[i], 0.0) for i in range(Z)], axis=0).astype(BF16)
+    held = dot(digits, jnp.where((iota((128, 128), 0) & 7) == iota((128, 128), 1), 1.0, 0.0).astype(BF16))
     wave = iota((Z * Y, WAVES), 1).astype(F32)
     for c in range(CORES):
         rows = jnp.zeros((Z * Y, 128), F32)
@@ -255,40 +262,46 @@
         to_band(z, *target)
     sent.append((3, row_out.at[pl.ds(0, BANDS - 1)]))
     row_in[band] = row_out[core * (Z * Y) + z * Y + y]
-    loads[4].wait()
+    loads[7].wait()
     wait_recv(3, row_in.at[pl.ds(0, BANDS - 1)])
 
     rows = row_in[...].reshape(BANDS, 128).T[:64]
     slot = legendre_row_of(iota((64, BANDS), 0))
-    total = jnp.zeros((64, WAVES), F32)
-    for s in range(4):
-        total = total + dot(jnp.where(slot == s, rows, 0.0).astype(BF16), p_in[s])
-    part_out[...] = total.reshape(LON, 16, WAVES).astype(BF16)
-    exchange(4, LON, to_lon, lambda o: part_out.at[over_lon(o)], part_in.at[lon], part_out)
-    part_in[lon] = part_out[lon]
-    wait_recv(4, part_in.at[pl.ds(0, LON - 1)])
+    own_slot = [jnp.where(slot == s, rows, 0.0).astype(BF16) for s in range(4)]
+    for n in range(WAVES // BLOCK):
+        total = dot(own_slot[0], p_in[0, :, n * BLOCK : (n + 1) * BLOCK])
+        for s in range(1, 4):
+            total = total + dot(own_slot[s], p_in[s, :, n * BLOCK : (n + 1) * BLOCK])
+        part_out[n] = total.reshape(LON, 16, BLOCK).astype(BF16)
+        part = part_in.at[n]
+        exchange(4 + n, LON, to_lon, lambda o: part_out.at[n, over_lon(o)], part.at[lon], part_out.at[n])
+        part[lon] = part_out[n, lon]
 
     slot = legendre_row_of(iota((16, 1), 0))
     limit = jnp.zeros((16, 1), I32)
     for s in range(4):
         limit = jnp.where(slot == s, WAVES - orders[s], limit)
-    part = [part_in[i].astype(F32) for i in range(LON)]
-    summed = (part[0] + part[1]) + (part[2] + part[3])
-    out[...] = jnp.where(iota((16, WAVES), 1) < limit, summed, 0.0)
+    for n in range(WAVES // BLOCK):
+        wait_recv(4 + n, part_in.at[n, pl.ds(0, LON - 1)])
+        part = [part_in[n, i].astype(F32) for i in range(LON)]
+        summed = (part[0] + part[1]) + (part[2] + part[3])
+        out[:, n * BLOCK : (n + 1) * BLOCK] = jnp.where(n * BLOCK + iota((16, BLOCK), 1) < limit, summed, 0.0)
 
     finish()
 
 
 def body(temperature, moisture, ground, operator, polynomial, latitudes, orders, layers):
     anywhere = pl.BlockSpec(memory_space=pl.ANY)
-    scalars = pl.BlockSpec(memory_space=pltpu.SMEM)
     vmem = pltpu.VMEM
     flat = pl.pallas_call(
         kernel,
         out_shape=jax.ShapeDtypeStruct((16, WAVES), F32),
-        in_specs=[scalars] * 3 + [anywhere] * 5,
+        in_specs=[anywhere] * 8,
         out_specs=pl.BlockSpec(memory_space=pltpu.VMEM),
         scratch_shapes=[
+            pltpu.SMEM(latitudes.shape, I32),
+            pltpu.SMEM(orders.shape, I32),
+            pltpu.SMEM(layers.shape, I32),
             vmem(temperature.shape, BF16),
             vmem(moisture.shape, BF16),
             vmem(ground.shape, BF16),
@@ -297,18 +310,18 @@
             vmem((4, LEVELS, 2 * HALF), F32),
             vmem((LON, 16, HALF), BF16),
             vmem((LON, 16, HALF), BF16),
-            vmem((YC, 8, 128), F32),
-            vmem((Z, 8, 128), F32),
+            vmem((YC, 1, 128), F32),
+            vmem((Z, 1, 128), F32),
             vmem((WAVES // 128, BLOCK, 256), BF16),
             vmem((WAVES // 128, BLOCKS, 256), F32),
             vmem((4, WAVES, 128), BF16),
             vmem((BANDS, 1, 128), F32),
             vmem((BANDS, 1, 128), F32),
-            vmem((LON, 16, WAVES), BF16),
-            vmem((LON, 16, WAVES), BF16),
-            pltpu.SemaphoreType.DMA((5,)),
-            pltpu.SemaphoreType.DMA((5,)),
-            pltpu.SemaphoreType.DMA((5,)),
+            vmem((WAVES // BLOCK, LON, 16, BLOCK), BF16),
+            vmem((WAVES // BLOCK, LON, 16, BLOCK), BF16),
+            pltpu.SemaphoreType.DMA((8,)),
+            pltpu.SemaphoreType.DMA((7,)),
+            pltpu.SemaphoreType.DMA((7,)),
         ],
         compiler_params=pltpu.CompilerParams(
             collective_id=0, has_side_effects=True, vmem_limit_bytes=60 * 1024 * 1024

time: 45.3 us -> 44.3 us (0.978)
  Pallas kernels: 43.7 us -> 42.6 us
    pallas_call x1, Pallas kernels: 43.7 us -> 42.6 us  [body(): pl.pallas_call(kernel, out_shape=jax.ShapeDtypeStruct((16, WAVES), F32),...]
where the time goes in v4:
time: 44.3 us; the launch traced here: 44.1 us
  Pallas kernels  42.6 us (96%)
  local copies, waits for them, and re-layouts  1.45 us (3%)
    pallas_call x1, Pallas kernels, body(): pl.pallas_call(kernel, out_shape=jax.ShapeDtypeStruct((16, WAVES), F32),...  42.6 us
    reshape x1, local copies, waits for them, and re-layouts, body(): return flat.reshape(4, 2, 2, WAVES)  1.45 us

profile of v4, /device:TPU:1, one launch (start us, length us, event | category | flops | bytes accessed | tf_op | source)
XLA Modules:
  0.0 44.1 jit_solution(7683914180630622540)
XLA Ops:
  0.0 42.6 %shard_map.82 = f32[16,768]{1,0:T(8,128)} custom-call(s32[4]{0:T(128)} %latitudes_at.1, s32[4]{0:T(128)} %orders_at.1, s32[8]{0:T(128)} %layers_at.1, bf16[4,8,1284]{2,1,0:T(8,128)(2,1)} %temperature.1, bf16[4,8,1284]{2,1,0:T(8,128)(2,1)} %moisture.1, bf16[4,1284]{1,0:T(4,128)(2,1)} %ground.1, f32[8,8]{1,0:T(8,128)} %operator.1, ...), custom_call_target="tpu_custom_call" | custom-call | tf_op jit(solution)/shard_map/pallas_call | solution.py:296
  42.6 1.4 %reshape.3 = f32[4,2,2,768]{3,2,1,0:T(2,128)} reshape(f32[16,768]{1,0:T(8,128)} %shard_map.82) | data formatting | bytes 98304 | tf_op jit(solution)/shard_map/reshape | solution.py:330

commit v5 on v4

--- a/solution.py
+++ b/solution.py
@@ -324,9 +324,9 @@
             pltpu.SemaphoreType.DMA((7,)),
         ],
         compiler_params=pltpu.CompilerParams(
-            collective_id=0, has_side_effects=True, vmem_limit_bytes=60 * 1024 * 1024
+            collective_id=0, has_side_effects=True, vmem_limit_bytes=32 * 1024 * 1024
         ),
-    )(latitudes, orders, layers, temperature, moisture, ground, operator, polynomial)
+    )(*[pltpu.with_memory_space_constraint(v, pltpu.HBM) for v in (latitudes, orders, layers, temperature, moisture, ground, operator, polynomial)])
     return flat.reshape(4, 2, 2, WAVES)
 
 

time: 44.3 us -> 42.8 us (0.966)
  local copies, waits for them, and re-layouts: 1.45 us -> 0.65 us
  Pallas kernels: 42.6 us -> 42 us
    reshape x1, local copies, waits for them, and re-layouts: 1.45 us -> 0.65 us  [body(): return flat.reshape(4, 2, 2, WAVES)]
    pallas_call x1, Pallas kernels: 42.6 us -> 42 us  [body(): pl.pallas_call(kernel, out_shape=jax.ShapeDtypeStruct((16, WAVES), F32),...]
where the time goes in v5:
time: 42.8 us; the launch traced here: 42.7 us
  Pallas kernels  42 us (98%)
  local copies, waits for them, and re-layouts  0.65 us (2%)
    pallas_call x1, Pallas kernels, body(): pl.pallas_call(kernel, out_shape=jax.ShapeDtypeStruct((16, WAVES), F32),...  42 us

profile of v5, /device:TPU:1, one launch (start us, length us, event | category | flops | bytes accessed | tf_op | source)
XLA Modules:
  0.0 42.7 jit_solution(7772908749311107489)
XLA Ops:
  0.0 42.0 %shard_map.82 = f32[16,768]{1,0:T(8,128)S(1)} custom-call(s32[4]{0:T(128)} %latitudes_at.1, s32[4]{0:T(128)} %orders_at.1, s32[8]{0:T(128)} %layers_at.1, bf16[4,8,1284]{2,1,0:T(8,128)(2,1)} %temperature.1, bf16[4,8,1284]{2,1,0:T(8,128)(2,1)} %moisture.1, bf16[4,1284]{1,0:T(4,128)(2,1)} %ground.1, f32[8,8]{1,0:T(8,128)} %operator.1, ...), custom_call_target="tpu_custom_call" | custom-call | tf_op jit(solution)/shard_map/pallas_call | solution.py:296
  42.0 0.7 %reshape.3 = f32[4,2,2,768]{3,2,1,0:T(2,128)} reshape(f32[16,768]{1,0:T(8,128)S(1)} %shard_map.82) | data formatting | bytes 98304 | tf_op jit(solution)/shard_map/reshape | solution.py:330
